TPU v7x, 512 devices: a whole 4x8x8 slice. The times are simulated.
512 devices in a mesh: seq: 64 (over z_lo, y, core), head: 8 (over z_hi, x).
Axes of the slice: x: 4, y: 8, z: 8 (z_hi: 2, z_lo: 4; z = z_hi * 4 + z_lo), core: 2. Of those that a mesh axis runs over, the one named last changes fastest.
Arguments:
- queries: bfloat16 [8192, 64, 128], P('seq', 'head'), may hold values from -11 to 11
- key_heads: bfloat16 [8192, 8, 128], P('seq', 'head'), may hold values from -20 to 20
- value_heads: bfloat16 [8192, 8, 128], P('seq', 'head'), may hold values from -6 to 6
- fold_map: int32 [64], replicated, may hold values from 0 to 63, as said below
- partner_map: int32 [2, 64], replicated, may hold values from 0 to 63, as said below
- out_weight: bfloat16 [8192, 5120], P('head', 'seq'), may hold values from -0.1875 to 0.1875
Outputs:
- projected: bfloat16 [8192, 5120], P('seq', 'head')
Inputs may be any that keep to these rules, and one draw needn't show every extreme that they name: `fold_map`: a permutation of 0 to 63. `partner_map`: round r pairs index i with index i XOR m_r, where m_r is nonzero and the two rounds have different m_r.
All inputs are finite; a program needn't handle non-finite values.
Results may differ from a plain program's by a relative error of at most 0.0051.
Values may be sent and summed in bfloat16 or wider, within the bound.
A program may use at most 64 MiB of HBM per device.

v0:
```python
import math
import jax
import jax.numpy as jnp
from jax import lax
from jax.sharding import PartitionSpec as P


def from_partner(shard, axis, distance):
    return lax.ppermute(shard, axis, [(i, i ^ 1 << distance) for i in range(lax.axis_size(axis))])


def per_device(queries, key_heads, value_heads, fold_map, partner_map, out_weight):
    my_index = lax.axis_index("seq")
    seq_count = lax.axis_size("seq")
    half_rows = queries.shape[0] // 2
    all_rows = 2 * half_rows
    local_kv = key_heads.shape[1]
    group_size = queries.shape[1] // local_kv
    head_dim = queries.shape[2]
    score_scale = 1.0 / math.sqrt(head_dim)
    query_groups = queries.reshape(all_rows, local_kv, group_size, head_dim)
    offsets = jnp.arange(half_rows, dtype=jnp.int32)

    def places_of(device):
        lower_block = fold_map[device]
        return jnp.concatenate(
            [
                lower_block * half_rows + offsets,
                (2 * seq_count - 1 - lower_block) * half_rows + offsets,
            ]
        )

    def raw_scores(query_part, key_part):
        return (
            jnp.einsum("rhje,khe->hjrk", query_part, key_part, preferred_element_type=jnp.float32)
            * score_scale
        )

    def weighted_sum(weights, value_part):
        return jnp.einsum(
            "hjrk,khe->rhje",
            weights.astype(jnp.bfloat16),
            value_part,
            preferred_element_type=jnp.float32,
        )

    my_places = places_of(my_index)
    own_scores = jnp.where(
        my_places[None, :] <= my_places[:, None], raw_scores(query_groups, key_heads), -jnp.inf
    )
    partner_a = partner_map[0, my_index]
    partner_b = partner_map[1, my_index]
    flip_a = jnp.bitwise_xor(partner_a, my_index)
    flip_b = jnp.bitwise_xor(partner_b, my_index)
    bit_count = seq_count.bit_length() - 1
    own_pair = jnp.stack([key_heads, value_heads])

    def route_pair(flip_mask):
        moving = own_pair
        for bit_index in range(bit_count):
            arrived = from_partner(moving, "seq", bit_index)
            take_this = jnp.bitwise_and(jnp.right_shift(flip_mask, bit_index), 1) == 1
            moving = jnp.where(take_this, arrived, moving)
        return moving

    pair_a = route_pair(flip_a)
    pair_b = route_pair(flip_b)
    own_max = jnp.max(own_scores, axis=-1)
    remote = []
    row_max = own_max
    for partner, moved_pair in ((partner_a, pair_a), (partner_b, pair_b)):
        their_places = places_of(partner)
        scores = jnp.where(
            their_places[None, :] <= my_places[:, None],
            raw_scores(query_groups, moved_pair[0]),
            -jnp.inf,
        )
        row_max = jnp.maximum(row_max, jnp.max(scores, axis=-1))
        remote.append((scores, moved_pair[1]))
    own_weights = jnp.exp(own_scores - row_max[..., None])
    row_total = jnp.sum(own_weights, axis=-1)
    weighted = weighted_sum(own_weights, value_heads)
    for scores, value_part in remote:
        weights = jnp.exp(scores - row_max[..., None])
        row_total = row_total + jnp.sum(weights, axis=-1)
        weighted = weighted + weighted_sum(weights, value_part)
    attended = (weighted / jnp.moveaxis(row_total, 2, 0)[..., None]).astype(jnp.bfloat16)
    flat_rows = attended.reshape(all_rows, local_kv * group_size * head_dim)
    partial_terms = jnp.dot(
        flat_rows,
        lax.all_gather(out_weight, "seq", axis=1, tiled=True),
        preferred_element_type=jnp.float32,
    )
    return lax.psum_scatter(partial_terms, "head", scatter_dimension=1, tiled=True).astype(
        jnp.bfloat16
    )


def solution(mesh):
    return jax.shard_map(
        per_device,
        mesh=mesh,
        in_specs=(
            P("seq", "head", None),
            P("seq", "head", None),
            P("seq", "head", None),
            P(),
            P(),
            P("head", "seq"),
        ),
        out_specs=P("seq", "head"),
        check_vma=False,
    )
```

profile of v0, /device:TPU:8, one launch (start us, length us, event | category | flops | bytes accessed | tf_op | source)
XLA Modules:
  0.0 270.4 jit_solution(317472850337719558)
XLA Ops:
  6.5 0.7 all-gather.2.cloned.1.call-update
  7.3 0.8 pad_maximum_fusion
  8.1 1.9 collective-permute-start
  10.0 1.4 constant_dynamic-slice_fusion.1
  15.2 1.4 fusion.31
  21.8 0.8 broadcast_select_fusion.6
  22.6 7.7 %collective-permute-start.1 = (bf16[2,128,1,128]{3,1,2,0:T(8,128)(2,1)S(1)}, bf16[2,128,1,128]{3,1,2,0:T(8,128)(2,1)S(1)}, u32[]{:S(2)}, u32[]{:S(2)}) collective-permute-start(bf16[2,128,1,128]{3,1,2,0:T(8,128)(2,1)S(1)} %get-tuple-element.8), channel_id=1, source_target_pairs={{0,16},{8,24},{16,0},{24,8},{32,48},{40,56},{48,32},{56,40},{64,80... | collective-permute-start | bytes 196616 | tf_op jit(solution)/shard_map/ppermute | solution.py:9
  30.3 1.0 fusion.33
  31.4 1.9 collective-permute-start.6
  33.3 0.3 collective-permute-done.1
  33.6 1.9 collective-permute-start.2
  35.6 3.4 %collective-permute-done.6 = bf16[2,128,1,128]{3,1,2,0:T(8,128)(2,1)S(1)} collective-permute-done((bf16[2,128,1,128]{3,1,2,0:T(8,128)(2,1)S(1)}, bf16[2,128,1,128]{3,1,2,0:T(8,128)(2,1)S(1)}, u32[]{:S(2)}, u32[]{:S(2)}) %collective-permute-start.6) | collective-permute-done | bytes 65568 | tf_op jit(solution)/shard_map/ppermute | solution.py:9
  39.0 1.9 collective-permute-start.7
  40.9 1.1 collective-permute-done.2
  42.0 1.9 collective-permute-start.3
  44.0 2.9 %collective-permute-done.7 = bf16[2,128,1,128]{3,1,2,0:T(8,128)(2,1)S(1)} collective-permute-done((bf16[2,128,1,128]{3,1,2,0:T(8,128)(2,1)S(1)}, bf16[2,128,1,128]{3,1,2,0:T(8,128)(2,1)S(1)}, u32[]{:S(2)}, u32[]{:S(2)}) %collective-permute-start.7) | collective-permute-done | bytes 65568 | tf_op jit(solution)/shard_map/ppermute | solution.py:9
  46.9 5.0 %collective-permute-start.8 = (bf16[2,128,1,128]{3,1,2,0:T(8,128)(2,1)S(1)}, bf16[2,128,1,128]{3,1,2,0:T(8,128)(2,1)S(1)}, u32[]{:S(2)}, u32[]{:S(2)}) collective-permute-start(bf16[2,128,1,128]{3,1,2,0:T(8,128)(2,1)S(1)} %broadcast_select_fusion.2), channel_id=1, source_target_pairs={{0,64},{8,72},{16,80},{24,88},{32,96},{40,104},{48,112},{56,120},{... | collective-permute-start | bytes 196616 | tf_op jit(solution)/shard_map/ppermute | solution.py:9
  51.8 1.8 collective-permute-done.3
  53.6 1.9 collective-permute-start.4
  55.5 3.6 %collective-permute-done.8 = bf16[2,128,1,128]{3,1,2,0:T(8,128)(2,1)S(1)} collective-permute-done((bf16[2,128,1,128]{3,1,2,0:T(8,128)(2,1)S(1)}, bf16[2,128,1,128]{3,1,2,0:T(8,128)(2,1)S(1)}, u32[]{:S(2)}, u32[]{:S(2)}) %collective-permute-start.8) | collective-permute-done | bytes 65568 | tf_op jit(solution)/shard_map/ppermute | solution.py:9
  59.1 1.9 collective-permute-start.9
  61.1 6.5 %collective-permute-start.5 = (bf16[2,128,1,128]{3,1,2,0:T(8,128)(2,1)S(1)}, bf16[2,128,1,128]{3,1,2,0:T(8,128)(2,1)S(1)}, u32[]{:S(2)}, u32[]{:S(2)}) collective-permute-start(bf16[2,128,1,128]{3,1,2,0:T(8,128)(2,1)S(1)} %broadcast_select_fusion.10), channel_id=1, source_target_pairs={{0,256},{8,264},{16,272},{24,280},{32,288},{40,296},{48,304},{56,3... | collective-permute-start | bytes 196616 | tf_op jit(solution)/shard_map/ppermute | solution.py:9
  67.6 2.2 collective-permute-start.10
  69.7 3.3 %collective-permute-done.5 = bf16[2,128,1,128]{3,1,2,0:T(8,128)(2,1)S(1)} collective-permute-done((bf16[2,128,1,128]{3,1,2,0:T(8,128)(2,1)S(1)}, bf16[2,128,1,128]{3,1,2,0:T(8,128)(2,1)S(1)}, u32[]{:S(2)}, u32[]{:S(2)}) %collective-permute-start.5) | collective-permute-done | bytes 65568 | tf_op jit(solution)/shard_map/ppermute | solution.py:9
  73.1 3.0 %collective-permute-done.10 = bf16[2,128,1,128]{3,1,2,0:T(8,128)(2,1)S(1)} collective-permute-done((bf16[2,128,1,128]{3,1,2,0:T(8,128)(2,1)S(1)}, bf16[2,128,1,128]{3,1,2,0:T(8,128)(2,1)S(1)}, u32[]{:S(2)}, u32[]{:S(2)}) %collective-permute-start.10) | collective-permute-done | bytes 65568 | tf_op jit(solution)/shard_map/ppermute | solution.py:9
  76.9 0.2 fusion.17
  77.2 1.0 convolution_bitcast_fusion
  78.2 0.3 fusion.9
  78.5 66.9 %all-gather.2.cloned.1.call-done = bf16[1024,5120]{0,1:T(8,128)(2,1)} async-done(((bf16[1024,80]{0,1:T(8,128)(2,1)}), bf16[1024,5120]{0,1:T(8,128)(2,1)}) %all-gather.2.cloned.1.call-update) | async-done | bytes 10485776 | tf_op jit(solution)/shard_map/all_gather | solution.py:91
  145.4 9.1 %fusion.35 = f32[128,5120]{1,0:T(8,128)} fusion(bf16[128,1024]{0,1:T(8,128)(2,1)S(1)} %bitcast.95, bf16[1024,5120]{0,1:T(8,128)(2,1)} %all-gather.2.cloned.1.call-done), kind=kOutput, calls=%fused_computation.73 | convolution fusion | flops 1342177280 | bytes 13369344 | tf_op jit(solution)/shard_map/dot_general | solution.py:89
  154.5 107.4 %reduce-scatter.2.cloned.1.call-done = f32[128,640]{1,0:T(8,128)} async-done(((f32[128,5120]{1,0:T(8,128)}), f32[128,640]{1,0:T(8,128)}) %reduce-scatter.2.cloned.1.call-update) | async-done | bytes 327696 | tf_op jit(solution)/shard_map/reduce_scatter | solution.py:94
  261.9 1.7 convert_element_type.19
  (30 shorter events, 1.3 us)
Async XLA Ops:
  6.5 23.8 %copy-start = (bf16[128,8,128]{2,1,0:T(8,128)(2,1)S(1)}, bf16[128,8,128]{2,1,0:T(8,128)(2,1)}, u32[]{:S(2)}) copy-start(bf16[128,8,128]{2,1,0:T(8,128)(2,1)} %param.6) | copy-start | bytes 786436
  6.5 138.8 %all-gather.2.cloned.1.call-start = ((), (), s32[]{:S(2)}) async-start(), calls=%async_computation.1 | async-start | bytes 10649600 | tf_op jit(solution)/shard_map/all_gather | solution.py:91
  7.3 254.7 %reduce-scatter.2.cloned.1.call-start = ((), (), s32[]{:S(2)}) async-start(), calls=%async_computation.2 | async-start | bytes 2949120 | tf_op jit(solution)/shard_map/reduce_scatter | solution.py:94
  8.1 13.7 %collective-permute-start = (bf16[2,128,1,128]{3,1,2,0:T(8,128)(2,1)S(1)}, bf16[2,128,1,128]{3,1,2,0:T(8,128)(2,1)S(1)}, u32[]{:S(2)}, u32[]{:S(2)}) collective-permute-start(bf16[2,128,1,128]{3,1,2,0:T(8,128)(2,1)S(1)} %pad_maximum_fusion), channel_id=1, source_target_pairs={{0,8},{8,0},{16,24},{24,16},{32,40},{40,32},{48,56},{56,48},{64,72... | collective-permute-start | bytes 196616 | tf_op jit(solution)/shard_map/ppermute | solution.py:9
  22.6 11.0 %collective-permute-start.1 = (bf16[2,128,1,128]{3,1,2,0:T(8,128)(2,1)S(1)}, bf16[2,128,1,128]{3,1,2,0:T(8,128)(2,1)S(1)}, u32[]{:S(2)}, u32[]{:S(2)}) collective-permute-start(bf16[2,128,1,128]{3,1,2,0:T(8,128)(2,1)S(1)} %get-tuple-element.8), channel_id=1, source_target_pairs={{0,16},{8,24},{16,0},{24,8},{32,48},{40,56},{48,32},{56,40},{64,80... | collective-permute-start | bytes 196616 | tf_op jit(solution)/shard_map/ppermute | solution.py:9
  31.4 7.6 %collective-permute-start.6 = (bf16[2,128,1,128]{3,1,2,0:T(8,128)(2,1)S(1)}, bf16[2,128,1,128]{3,1,2,0:T(8,128)(2,1)S(1)}, u32[]{:S(2)}, u32[]{:S(2)}) collective-permute-start(bf16[2,128,1,128]{3,1,2,0:T(8,128)(2,1)S(1)} %get-tuple-element.9), channel_id=1, source_target_pairs={{0,16},{8,24},{16,0},{24,8},{32,48},{40,56},{48,32},{56,40},{64,80... | collective-permute-start | bytes 196616 | tf_op jit(solution)/shard_map/ppermute | solution.py:9
  33.6 8.4 %collective-permute-start.2 = (bf16[2,128,1,128]{3,1,2,0:T(8,128)(2,1)S(1)}, bf16[2,128,1,128]{3,1,2,0:T(8,128)(2,1)S(1)}, u32[]{:S(2)}, u32[]{:S(2)}) collective-permute-start(bf16[2,128,1,128]{3,1,2,0:T(8,128)(2,1)S(1)} %broadcast_select_fusion.7), channel_id=1, source_target_pairs={{0,32},{8,40},{16,48},{24,56},{32,0},{40,8},{48,16},{56,24},{64,96... | collective-permute-start | bytes 196616 | tf_op jit(solution)/shard_map/ppermute | solution.py:9
  39.0 7.8 %collective-permute-start.7 = (bf16[2,128,1,128]{3,1,2,0:T(8,128)(2,1)S(1)}, bf16[2,128,1,128]{3,1,2,0:T(8,128)(2,1)S(1)}, u32[]{:S(2)}, u32[]{:S(2)}) collective-permute-start(bf16[2,128,1,128]{3,1,2,0:T(8,128)(2,1)S(1)} %broadcast_select_fusion.1), channel_id=1, source_target_pairs={{0,32},{8,40},{16,48},{24,56},{32,0},{40,8},{48,16},{56,24},{64,96... | collective-permute-start | bytes 196616 | tf_op jit(solution)/shard_map/ppermute | solution.py:9
  42.0 11.6 %collective-permute-start.3 = (bf16[2,128,1,128]{3,1,2,0:T(8,128)(2,1)S(1)}, bf16[2,128,1,128]{3,1,2,0:T(8,128)(2,1)S(1)}, u32[]{:S(2)}, u32[]{:S(2)}) collective-permute-start(bf16[2,128,1,128]{3,1,2,0:T(8,128)(2,1)S(1)} %broadcast_select_fusion.8), channel_id=1, source_target_pairs={{0,64},{8,72},{16,80},{24,88},{32,96},{40,104},{48,112},{56,120},{... | collective-permute-start | bytes 196616 | tf_op jit(solution)/shard_map/ppermute | solution.py:9
  46.9 12.2 %collective-permute-start.8 = (bf16[2,128,1,128]{3,1,2,0:T(8,128)(2,1)S(1)}, bf16[2,128,1,128]{3,1,2,0:T(8,128)(2,1)S(1)}, u32[]{:S(2)}, u32[]{:S(2)}) collective-permute-start(bf16[2,128,1,128]{3,1,2,0:T(8,128)(2,1)S(1)} %broadcast_select_fusion.2), channel_id=1, source_target_pairs={{0,64},{8,72},{16,80},{24,88},{32,96},{40,104},{48,112},{56,120},{... | collective-permute-start | bytes 196616 | tf_op jit(solution)/shard_map/ppermute | solution.py:9
  53.6 7.4 %collective-permute-start.4 = (bf16[2,128,1,128]{3,1,2,0:T(8,128)(2,1)S(1)}, bf16[2,128,1,128]{3,1,2,0:T(8,128)(2,1)S(1)}, u32[]{:S(2)}, u32[]{:S(2)}) collective-permute-start(bf16[2,128,1,128]{3,1,2,0:T(8,128)(2,1)S(1)} %broadcast_select_fusion.9), channel_id=1, source_target_pairs={{0,128},{8,136},{16,144},{24,152},{32,160},{40,168},{48,176},{56,1... | collective-permute-start | bytes 196616 | tf_op jit(solution)/shard_map/ppermute | solution.py:9
  59.1 8.4 %collective-permute-start.9 = (bf16[2,128,1,128]{3,1,2,0:T(8,128)(2,1)S(1)}, bf16[2,128,1,128]{3,1,2,0:T(8,128)(2,1)S(1)}, u32[]{:S(2)}, u32[]{:S(2)}) collective-permute-start(bf16[2,128,1,128]{3,1,2,0:T(8,128)(2,1)S(1)} %broadcast_select_fusion.3), channel_id=1, source_target_pairs={{0,128},{8,136},{16,144},{24,152},{32,160},{40,168},{48,176},{56,1... | collective-permute-start | bytes 196616 | tf_op jit(solution)/shard_map/ppermute | solution.py:9
  61.1 12.0 %collective-permute-start.5 = (bf16[2,128,1,128]{3,1,2,0:T(8,128)(2,1)S(1)}, bf16[2,128,1,128]{3,1,2,0:T(8,128)(2,1)S(1)}, u32[]{:S(2)}, u32[]{:S(2)}) collective-permute-start(bf16[2,128,1,128]{3,1,2,0:T(8,128)(2,1)S(1)} %broadcast_select_fusion.10), channel_id=1, source_target_pairs={{0,256},{8,264},{16,272},{24,280},{32,288},{40,296},{48,304},{56,3... | collective-permute-start | bytes 196616 | tf_op jit(solution)/shard_map/ppermute | solution.py:9
  67.6 8.6 %collective-permute-start.10 = (bf16[2,128,1,128]{3,1,2,0:T(8,128)(2,1)S(1)}, bf16[2,128,1,128]{3,1,2,0:T(8,128)(2,1)S(1)}, u32[]{:S(2)}, u32[]{:S(2)}) collective-permute-start(bf16[2,128,1,128]{3,1,2,0:T(8,128)(2,1)S(1)} %broadcast_select_fusion.4), channel_id=1, source_target_pairs={{0,256},{8,264},{16,272},{24,280},{32,288},{40,296},{48,304},{56,3... | collective-permute-start | bytes 196616 | tf_op jit(solution)/shard_map/ppermute | solution.py:9
Sparse Core Ops, SparseCore 0:
  9.5 135.8 all-gather.1
  154.7 107.2 reduce-scatter.1
where the time goes:
time: 271 us; the launch traced here: 270 us
  waiting for transfers between devices  194 us (72%)
  starting transfers between devices  34.8 us (13%)
  between operations  22.3 us (8%)
  matrix products  12.2 us (5%)
  other arithmetic  3.94 us (1%)
  local copies, waits for them, and re-layouts  2.74 us (1%)
    reduce_scatter x1, waiting for transfers between devices, per_device(): lax.psum_scatter(partial_terms, 'head', scatter_dimension=1, tiled=True)  107 us
    all_gather x1, waiting for transfers between devices, per_device(): lax.all_gather(out_weight, 'seq', axis=1, tiled=True)  66.9 us
    ppermute x11, starting transfers between devices, from_partner(): lax.ppermute(shard, axis, [(i, i ^ 1 << distance) for i in range(lax.axis...  34.8 us
    ppermute x11, waiting for transfers between devices, from_partner(): lax.ppermute(shard, axis, [(i, i ^ 1 << distance) for i in range(lax.axis...  19.4 us
    dot_general x1, matrix products, per_device(): jnp.dot(flat_rows, lax.all_gather(out_weight, 'seq', axis=1, tiled=True),...  9.14 us
  transfers between devices with their start and end apart: 13, of which 10 were waited for; matrix products, arithmetic and copies ran while one was open for 3% of the time, Pallas kernels for 0%

commit v1 on v0

--- a/solution.py
+++ b/solution.py
@@ -88,7 +88,9 @@
     flat_rows = attended.reshape(all_rows, local_kv * group_size * head_dim)
     partial_terms = jnp.dot(
         flat_rows,
-        lax.all_gather(out_weight, "seq", axis=1, tiled=True),
+        jnp.concatenate(
+            lax.all_to_all(jnp.stack([out_weight] * lax.axis_size("seq")), "seq", 0, 0), axis=1
+        ),
         preferred_element_type=jnp.float32,
     )
     return lax.psum_scatter(partial_terms, "head", scatter_dimension=1, tiled=True).astype(

time: 271 us -> 450 us (1.66)
  waiting for transfers between devices: 194 us -> 345 us
  starting transfers between devices: 34.8 us -> 60.2 us
  local copies, waits for them, and re-layouts: 2.74 us -> 7.49 us
    ppermute x11, waiting for transfers between devices: 19.4 us -> 235 us  [from_partner(): lax.ppermute(shard, axis, [(i, i ^ 1 << distance) for i in range(lax.axis...]
    all_gather x1 -> x0, waiting for transfers between devices: 66.9 us -> none  [per_device(): lax.all_gather(out_weight, 'seq', axis=1, tiled=True)]
    all_to_all x0 -> x1, starting transfers between devices: none -> 13.8 us  [per_device(): lax.all_to_all(jnp.stack([out_weight] * lax.axis_size('seq')), 'seq', 0, 0)]
    ppermute x11, starting transfers between devices: 34.8 us -> 46.3 us  [from_partner(): lax.ppermute(shard, axis, [(i, i ^ 1 << distance) for i in range(lax.axis...]
    another operation x0 -> x1, local copies, waits for them, and re-layouts: none -> 6.12 us  [per_device(): jnp.stack([out_weight] * lax.axis_size('seq'))]
  transfers between devices with their start and end apart: 13 -> 13, of which waited for: 10 -> 8; matrix products, arithmetic and copies ran while one was open for 3% -> 1% of each run, Pallas kernels for 0% -> 0%
where the time goes in v1:
time: 450 us; the launch traced here: 449 us
  waiting for transfers between devices  345 us (77%)
  starting transfers between devices  60.2 us (13%)
  between operations  22.9 us (5%)
  matrix products  10.6 us (2%)
  local copies, waits for them, and re-layouts  7.49 us (2%)
    ppermute x11, waiting for transfers between devices, from_partner(): lax.ppermute(shard, axis, [(i, i ^ 1 << distance) for i in range(lax.axis...  235 us
    reduce_scatter x1, waiting for transfers between devices, per_device(): lax.psum_scatter(partial_terms, 'head', scatter_dimension=1, tiled=True)  110 us
    ppermute x11, starting transfers between devices, from_partner(): lax.ppermute(shard, axis, [(i, i ^ 1 << distance) for i in range(lax.axis...  46.3 us
    all_to_all x1, starting transfers between devices, per_device(): lax.all_to_all(jnp.stack([out_weight] * lax.axis_size('seq')), 'seq', 0, 0)  13.8 us
    dot_general x1, matrix products, per_device(): jnp.dot(flat_rows, jnp.concatenate(lax.all_to_all(jnp.stack([out_weight]...  9.15 us
  transfers between devices with their start and end apart: 13, of which 8 were waited for; matrix products, arithmetic and copies ran while one was open for 1% of the time, Pallas kernels for 0%

profile of v1, /device:TPU:8, one launch (start us, length us, event | category | flops | bytes accessed | tf_op | source)
XLA Modules:
  0.0 448.8 jit_solution(10436931591715507929)
XLA Ops:
  6.5 6.1 %stack.11 = bf16[64,1024,80]{1,2,0:T(8,128)(2,1)} broadcast(bf16[1024,80]{0,1:T(8,128)(2,1)} %param.11), dimensions={1,2} | broadcast | bytes 10649600 | tf_op jit(solution)/shard_map/stack | solution.py:92
  12.7 13.8 %all-to-all-start = ((bf16[64,1024,80]{1,2,0:T(8,128)(2,1)}), bf16[64,1024,80]{1,2,0:T(8,128)(2,1)}, u32[]{:S(2)}, u32[]{:S(2)}) async-start(bf16[64,1024,80]{1,2,0:T(8,128)(2,1)} %stack.11), calls=%async_computation | async-start | bytes 20971520 | tf_op jit(solution)/shard_map/all_to_all | solution.py:92
  26.6 2.1 collective-permute-start
  28.7 0.7 constant_dynamic-slice_fusion.1
  33.4 0.7 fusion.31
  39.6 2.3 collective-permute-start.1
  41.9 0.2 fusion.33
  42.2 3.6 collective-permute-start.6
  45.8 226.4 %collective-permute-done.1 = bf16[2,128,1,128]{3,1,2,0:T(8,128)(2,1)S(1)} collective-permute-done((bf16[2,128,1,128]{3,1,2,0:T(8,128)(2,1)S(1)}, bf16[2,128,1,128]{3,1,2,0:T(8,128)(2,1)S(1)}, u32[]{:S(2)}, u32[]{:S(2)}) %collective-permute-start.1) | collective-permute-done | bytes 65568 | tf_op jit(solution)/shard_map/ppermute | solution.py:9
  272.1 9.8 %collective-permute-start.2 = (bf16[2,128,1,128]{3,1,2,0:T(8,128)(2,1)S(1)}, bf16[2,128,1,128]{3,1,2,0:T(8,128)(2,1)S(1)}, u32[]{:S(2)}, u32[]{:S(2)}) collective-permute-start(bf16[2,128,1,128]{3,1,2,0:T(8,128)(2,1)S(1)} %broadcast_select_fusion.7), channel_id=1, source_target_pairs={{0,32},{8,40},{16,48},{24,56},{32,0},{40,8},{48,16},{56,24},{64,96... | collective-permute-start | bytes 196616 | tf_op jit(solution)/shard_map/ppermute | solution.py:9
  282.0 1.9 collective-permute-start.7
  283.9 1.9 collective-permute-done.2
  285.8 1.9 collective-permute-start.3
  287.7 1.3 collective-permute-done.7
  289.0 6.6 %collective-permute-start.8 = (bf16[2,128,1,128]{3,1,2,0:T(8,128)(2,1)S(1)}, bf16[2,128,1,128]{3,1,2,0:T(8,128)(2,1)S(1)}, u32[]{:S(2)}, u32[]{:S(2)}) collective-permute-start(bf16[2,128,1,128]{3,1,2,0:T(8,128)(2,1)S(1)} %broadcast_select_fusion.2), channel_id=1, source_target_pairs={{0,64},{8,72},{16,80},{24,88},{32,96},{40,104},{48,112},{56,120},{... | collective-permute-start | bytes 196616 | tf_op jit(solution)/shard_map/ppermute | solution.py:9
  295.6 0.3 collective-permute-done.3
  295.9 1.9 collective-permute-start.4
  297.8 1.7 collective-permute-done.8
  299.6 2.2 collective-permute-start.9
  301.8 0.5 collective-permute-done.4
  302.3 10.1 %collective-permute-start.5 = (bf16[2,128,1,128]{3,1,2,0:T(8,128)(2,1)S(1)}, bf16[2,128,1,128]{3,1,2,0:T(8,128)(2,1)S(1)}, u32[]{:S(2)}, u32[]{:S(2)}) collective-permute-start(bf16[2,128,1,128]{3,1,2,0:T(8,128)(2,1)S(1)} %broadcast_select_fusion.10), channel_id=1, source_target_pairs={{0,256},{8,264},{16,272},{24,280},{32,288},{40,296},{48,304},{56,3... | collective-permute-start | bytes 196616 | tf_op jit(solution)/shard_map/ppermute | solution.py:9
  312.5 4.0 collective-permute-start.10
  316.5 3.2 collective-permute-done.10
  319.8 0.2 fusion.32
  320.0 0.2 fusion.34
  320.3 0.2 fusion.12
  320.5 0.2 fusion.17
  320.8 0.3 convolution_bitcast_fusion
  321.1 0.3 fusion.9
  321.3 9.2 %fusion.35 = f32[128,5120]{1,0:T(8,128)} fusion(bf16[128,1024]{0,1:T(8,128)(2,1)S(1)} %bitcast.98, bf16[1024,5120]{0,1:T(8,128)(2,1)} %bitcast.39), kind=kOutput, calls=%fused_computation.73 | convolution fusion | flops 1342177280 | bytes 13369344 | tf_op jit(solution)/shard_map/dot_general | solution.py:89
  330.5 109.8 %reduce-scatter.2.cloned.1.call-done = f32[128,640]{1,0:T(8,128)} async-done(((f32[128,5120]{1,0:T(8,128)}), f32[128,640]{1,0:T(8,128)}) %reduce-scatter.2.cloned.1.call-update) | async-done | bytes 327696 | tf_op jit(solution)/shard_map/reduce_scatter | solution.py:96
  440.3 1.7 convert_element_type.19
  (38 shorter events, 0.6 us)
Async XLA Ops:
  6.5 35.4 %copy-start = (bf16[128,8,128]{2,1,0:T(8,128)(2,1)S(1)}, bf16[128,8,128]{2,1,0:T(8,128)(2,1)}, u32[]{:S(2)}) copy-start(bf16[128,8,128]{2,1,0:T(8,128)(2,1)} %param.6) | copy-start | bytes 786436
  12.7 13.9 %copy-start.1 = (bf16[128,1,128]{2,0,1:T(8,128)(2,1)S(1)}, bf16[128,1,128]{2,0,1:T(8,128)(2,1)}, u32[]{:S(2)}) copy-start(bf16[128,1,128]{2,0,1:T(8,128)(2,1)} %param.7) | copy-start | bytes 98308
  12.7 13.9 %copy-start.2 = (bf16[128,1,128]{2,0,1:T(8,128)(2,1)S(1)}, bf16[128,1,128]{2,0,1:T(8,128)(2,1)}, u32[]{:S(2)}) copy-start(bf16[128,1,128]{2,0,1:T(8,128)(2,1)} %param.8) | copy-start | bytes 98308
  12.7 16.0 %copy-start.4 = (s32[2,64]{1,0:T(2,128)S(1)}, s32[2,64]{1,0:T(2,128)}, u32[]{:S(2)}) copy-start(s32[2,64]{1,0:T(2,128)} %param.10) | copy-start | bytes 1540
  12.7 20.7 %copy-start.3 = (s32[64]{0:T(128)S(1)}, s32[64]{0:T(128)}, u32[]{:S(2)}) copy-start(s32[64]{0:T(128)} %param.9) | copy-start | bytes 772
  12.7 308.7 %all-to-all-start = ((bf16[64,1024,80]{1,2,0:T(8,128)(2,1)}), bf16[64,1024,80]{1,2,0:T(8,128)(2,1)}, u32[]{:S(2)}, u32[]{:S(2)}) async-start(bf16[64,1024,80]{1,2,0:T(8,128)(2,1)} %stack.11), calls=%async_computation | async-start | bytes 20971520 | tf_op jit(solution)/shard_map/all_to_all | solution.py:92
  26.5 413.8 %reduce-scatter.2.cloned.1.call-start = ((), (), s32[]{:S(2)}) async-start(), calls=%async_computation.2 | async-start | bytes 2949120 | tf_op jit(solution)/shard_map/reduce_scatter | solution.py:96
  26.6 13.0 %collective-permute-start = (bf16[2,128,1,128]{3,1,2,0:T(8,128)(2,1)S(1)}, bf16[2,128,1,128]{3,1,2,0:T(8,128)(2,1)S(1)}, u32[]{:S(2)}, u32[]{:S(2)}) collective-permute-start(bf16[2,128,1,128]{3,1,2,0:T(8,128)(2,1)S(1)} %pad_maximum_fusion), channel_id=1, source_target_pairs={{0,8},{8,0},{16,24},{24,16},{32,40},{40,32},{48,56},{56,48},{64,72... | collective-permute-start | bytes 196616 | tf_op jit(solution)/shard_map/ppermute | solution.py:9
  39.6 232.5 %collective-permute-start.1 = (bf16[2,128,1,128]{3,1,2,0:T(8,128)(2,1)S(1)}, bf16[2,128,1,128]{3,1,2,0:T(8,128)(2,1)S(1)}, u32[]{:S(2)}, u32[]{:S(2)}) collective-permute-start(bf16[2,128,1,128]{3,1,2,0:T(8,128)(2,1)S(1)} %get-tuple-element.8), channel_id=1, source_target_pairs={{0,16},{8,24},{16,0},{24,8},{32,48},{40,56},{48,32},{56,40},{64,80... | collective-permute-start | bytes 196616 | tf_op jit(solution)/shard_map/ppermute | solution.py:9
  42.2 239.7 %collective-permute-start.6 = (bf16[2,128,1,128]{3,1,2,0:T(8,128)(2,1)S(1)}, bf16[2,128,1,128]{3,1,2,0:T(8,128)(2,1)S(1)}, u32[]{:S(2)}, u32[]{:S(2)}) collective-permute-start(bf16[2,128,1,128]{3,1,2,0:T(8,128)(2,1)S(1)} %get-tuple-element.9), channel_id=1, source_target_pairs={{0,16},{8,24},{16,0},{24,8},{32,48},{40,56},{48,32},{56,40},{64,80... | collective-permute-start | bytes 196616 | tf_op jit(solution)/shard_map/ppermute | solution.py:9
  272.1 13.6 %collective-permute-start.2 = (bf16[2,128,1,128]{3,1,2,0:T(8,128)(2,1)S(1)}, bf16[2,128,1,128]{3,1,2,0:T(8,128)(2,1)S(1)}, u32[]{:S(2)}, u32[]{:S(2)}) collective-permute-start(bf16[2,128,1,128]{3,1,2,0:T(8,128)(2,1)S(1)} %broadcast_select_fusion.7), channel_id=1, source_target_pairs={{0,32},{8,40},{16,48},{24,56},{32,0},{40,8},{48,16},{56,24},{64,96... | collective-permute-start | bytes 196616 | tf_op jit(solution)/shard_map/ppermute | solution.py:9
  282.0 7.1 %collective-permute-start.7 = (bf16[2,128,1,128]{3,1,2,0:T(8,128)(2,1)S(1)}, bf16[2,128,1,128]{3,1,2,0:T(8,128)(2,1)S(1)}, u32[]{:S(2)}, u32[]{:S(2)}) collective-permute-start(bf16[2,128,1,128]{3,1,2,0:T(8,128)(2,1)S(1)} %broadcast_select_fusion.1), channel_id=1, source_target_pairs={{0,32},{8,40},{16,48},{24,56},{32,0},{40,8},{48,16},{56,24},{64,96... | collective-permute-start | bytes 196616 | tf_op jit(solution)/shard_map/ppermute | solution.py:9
  285.8 10.1 %collective-permute-start.3 = (bf16[2,128,1,128]{3,1,2,0:T(8,128)(2,1)S(1)}, bf16[2,128,1,128]{3,1,2,0:T(8,128)(2,1)S(1)}, u32[]{:S(2)}, u32[]{:S(2)}) collective-permute-start(bf16[2,128,1,128]{3,1,2,0:T(8,128)(2,1)S(1)} %broadcast_select_fusion.8), channel_id=1, source_target_pairs={{0,64},{8,72},{16,80},{24,88},{32,96},{40,104},{48,112},{56,120},{... | collective-permute-start | bytes 196616 | tf_op jit(solution)/shard_map/ppermute | solution.py:9
  289.0 10.5 %collective-permute-start.8 = (bf16[2,128,1,128]{3,1,2,0:T(8,128)(2,1)S(1)}, bf16[2,128,1,128]{3,1,2,0:T(8,128)(2,1)S(1)}, u32[]{:S(2)}, u32[]{:S(2)}) collective-permute-start(bf16[2,128,1,128]{3,1,2,0:T(8,128)(2,1)S(1)} %broadcast_select_fusion.2), channel_id=1, source_target_pairs={{0,64},{8,72},{16,80},{24,88},{32,96},{40,104},{48,112},{56,120},{... | collective-permute-start | bytes 196616 | tf_op jit(solution)/shard_map/ppermute | solution.py:9
  295.9 6.4 %collective-permute-start.4 = (bf16[2,128,1,128]{3,1,2,0:T(8,128)(2,1)S(1)}, bf16[2,128,1,128]{3,1,2,0:T(8,128)(2,1)S(1)}, u32[]{:S(2)}, u32[]{:S(2)}) collective-permute-start(bf16[2,128,1,128]{3,1,2,0:T(8,128)(2,1)S(1)} %broadcast_select_fusion.9), channel_id=1, source_target_pairs={{0,128},{8,136},{16,144},{24,152},{32,160},{40,168},{48,176},{56,1... | collective-permute-start | bytes 196616 | tf_op jit(solution)/shard_map/ppermute | solution.py:9
  299.6 12.9 %collective-permute-start.9 = (bf16[2,128,1,128]{3,1,2,0:T(8,128)(2,1)S(1)}, bf16[2,128,1,128]{3,1,2,0:T(8,128)(2,1)S(1)}, u32[]{:S(2)}, u32[]{:S(2)}) collective-permute-start(bf16[2,128,1,128]{3,1,2,0:T(8,128)(2,1)S(1)} %broadcast_select_fusion.3), channel_id=1, source_target_pairs={{0,128},{8,136},{16,144},{24,152},{32,160},{40,168},{48,176},{56,1... | collective-permute-start | bytes 196616 | tf_op jit(solution)/shard_map/ppermute | solution.py:9
  302.3 14.2 %collective-permute-start.5 = (bf16[2,128,1,128]{3,1,2,0:T(8,128)(2,1)S(1)}, bf16[2,128,1,128]{3,1,2,0:T(8,128)(2,1)S(1)}, u32[]{:S(2)}, u32[]{:S(2)}) collective-permute-start(bf16[2,128,1,128]{3,1,2,0:T(8,128)(2,1)S(1)} %broadcast_select_fusion.10), channel_id=1, source_target_pairs={{0,256},{8,264},{16,272},{24,280},{32,288},{40,296},{48,304},{56,3... | collective-permute-start | bytes 196616 | tf_op jit(solution)/shard_map/ppermute | solution.py:9
  312.5 7.3 %collective-permute-start.10 = (bf16[2,128,1,128]{3,1,2,0:T(8,128)(2,1)S(1)}, bf16[2,128,1,128]{3,1,2,0:T(8,128)(2,1)S(1)}, u32[]{:S(2)}, u32[]{:S(2)}) collective-permute-start(bf16[2,128,1,128]{3,1,2,0:T(8,128)(2,1)S(1)} %broadcast_select_fusion.4), channel_id=1, source_target_pairs={{0,256},{8,264},{16,272},{24,280},{32,288},{40,296},{48,304},{56,3... | collective-permute-start | bytes 196616 | tf_op jit(solution)/shard_map/ppermute | solution.py:9
Sparse Core Ops, SparseCore 0:
  330.6 109.6 reduce-scatter.1
